TPU v7x, 32 devices: a whole 2x2x4 slice. The times are simulated.
32 devices in a mesh: leaf: 8 (over y, x, core), grp: 4 (over z).
Axes of the slice: x: 2, y: 2, z: 4, core: 2. Of those that a mesh axis runs over, the one named last changes fastest.
Arguments:
- root_inverse: float32 [512, 512], P(('leaf', 'grp'))
- child_tiles: int32 [8, 8], P('leaf'), may hold values from 0 to 7, as said below
- tile_valid: int32 [8, 8], P('leaf'), may hold values 0 or 1
- factor_off: float32 [8, 512, 512], P('leaf'), may hold values from -0.75 to 0.75
- diag_inverse_t: float32 [8, 512, 512], P('leaf', 'grp')
Outputs:
- cross_blocks: float32 [8, 512, 512], P('leaf', 'grp')
- diagonal_blocks: float32 [8, 512, 512], P('leaf', 'grp')
Inputs may be any that keep to these rules, and one draw needn't show every extreme that they name: `child_tiles`: each row lists 8 different tiles.
All inputs are finite; a program needn't handle non-finite values. No bound on the sum of `tile_valid` on one device may be relied on, other than what follows from the above.
Results may differ from a plain program's by a relative error of at most 0.0003.
Values sent between devices are 32-bit elements; how exact they have to be, the bound alone decides.
A program may use at most 128 MiB of HBM per device.

v0:
```python
import jax
import jax.numpy as jnp
from jax import lax
from jax.sharding import PartitionSpec as P

B = 64


def pick_block(source, tile_ids, tile_rows):
    highest = lax.Precision.HIGHEST
    tile_count = source.shape[1] // B
    children = tile_ids.shape[0]
    listed = tile_ids.shape[1]
    one_hot = (
        tile_ids[:, :, None] == jnp.arange(tile_count, dtype=jnp.int32)[None, None, :]
    ).astype(jnp.float32)
    flat_source = source.reshape(tile_count, tile_rows * tile_count * B)
    row_pick = jnp.einsum("ckt,tx->ckx", one_hot, flat_source, precision=highest)
    row_pick = row_pick.reshape(children, listed * tile_rows, tile_count, B)
    picked = jnp.einsum("crtb,cjt->crjb", row_pick, one_hot, precision=highest)
    return picked.reshape(children, listed * tile_rows, listed * B)


def on_device(root_inverse, child_tiles, tile_valid, factor_off, diag_inverse_t):
    highest = lax.Precision.HIGHEST
    row_mask = jnp.repeat(tile_valid.astype(jnp.float32), B, axis=1)
    masked_factor = factor_off * row_mask[:, :, None]
    whole_root = lax.all_gather(root_inverse, ("leaf", "grp"), axis=0, tiled=True)
    picked = pick_block(whole_root, child_tiles, B)
    product = jnp.einsum("crn,ckn->crk", diag_inverse_t, masked_factor, precision=highest)
    blocks = -jnp.einsum("crk,ckj->crj", product, picked, precision=highest) * row_mask[:, None, :]
    q_rows = diag_inverse_t - jnp.einsum("crk,ckn->crn", blocks, masked_factor, precision=highest)
    q_full = lax.all_gather(q_rows, "grp", axis=1, tiled=True)
    closing = jnp.einsum("crn,cmn->crm", diag_inverse_t, q_full, precision=highest)
    return (blocks, closing)


def solution(mesh):
    in_specs = (
        P(("leaf", "grp"), None),
        P("leaf", None),
        P("leaf", None),
        P("leaf", None, None),
        P("leaf", "grp", None),
    )
    out_specs = (P("leaf", "grp", None), P("leaf", "grp", None))
    return jax.shard_map(
        on_device, mesh=mesh, in_specs=in_specs, out_specs=out_specs, check_vma=False
    )
```

profile of v0, /device:TPU:0, one launch (start us, length us, event | category | flops | bytes accessed | tf_op | source)
XLA Modules:
  0.0 112.6 jit_solution(3488118699961421633)
XLA Ops:
  7.2 0.0 copy-start.3
  7.2 0.0 all-gather.3.cloned.1.call-start
  7.2 0.7 all-gather.3.cloned.1.call-update
  7.9 0.0 all-gather.5.cloned.1.call-start
  8.0 0.7 convert_bitcast_fusion
  8.6 0.1 broadcast_in_dim.7
  8.7 0.1 broadcast_in_dim.8
  8.8 2.3 %fusion.4 = f32[512,128]{1,0:T(8,128)S(1)} fusion(f32[1,512,512]{2,1,0:T(8,128)} %param.8, f32[512]{0:T(512)S(1)} %broadcast_in_dim.8, f32[1,128,512]{2,1,0:T(8,128)} %param.9), kind=kOutput, calls=%fused_computation.8 | convolution fusion | flops 402915328 | bytes 1574912 | tf_op jit(solution)/shard_map/crn,ckn->crk/dot_general | solution.py:30
  11.1 56.4 %all-gather.3.cloned.1.call-done = f32[512,512]{1,0:T(8,128)} async-done(((f32[16,512]{1,0:T(8,128)}), f32[512,512]{1,0:T(8,128)}) %all-gather.3.cloned.1.call-update) | async-done | bytes 1048592 | tf_op jit(solution)/shard_map/all_gather | solution.py:28
  67.5 1.4 %reshape.127 = f32[8,32768]{1,0:T(8,128)S(1)} reshape(f32[512,512]{1,0:T(8,128)} %all-gather.3.cloned.1.call-done) | data formatting | bytes 2097152 | tf_op jit(solution)/shard_map/reshape | solution.py:17
  68.9 0.0 copy-done.3
  68.9 0.6 fusion.14
  69.6 0.8 reshape.128
  70.4 1.2 %copy.9 = f32[512,8,64]{0,1,2:T(8,128)S(1)} copy(f32[512,8,64]{2,1,0:T(8,128)S(1)} %reshape.128) | data formatting | bytes 2097152 | tf_op jit(solution)/shard_map/reshape.16
  71.6 0.6 convolution_bitcast_fusion
  72.2 0.0 copy-start
  72.2 0.0 copy-start.1
  72.2 0.6 copy.10
  72.9 1.2 %fusion = f32[128,512]{1,0:T(8,128)S(1)} fusion(f32[512,128]{1,0:T(8,128)S(1)} %fusion.4, f32[512,512]{0,1:T(8,128)S(1)} %bitcast.42, f32[512]{0:T(512)S(1)} %broadcast_in_dim.8), kind=kOutput, calls=%fused_computation.4 | convolution fusion | flops 402784256 | bytes 1574912 | tf_op jit(solution)/shard_map/crk,ckj->crj/dot_general | solution.py:31
  74.1 0.0 copy-done
  74.1 0.0 copy-done.1
  74.1 0.0 copy-start.2
  74.2 1.5 %fusion.1 = f32[1,128,512]{2,1,0:T(8,128)} fusion(f32[1,128,512]{2,1,0:T(8,128)S(1)} %copy-done.1, f32[128,512]{1,0:T(8,128)S(1)} %fusion, f32[1,512,512]{2,1,0:T(8,128)S(1)} %copy-done, f32[512]{0:T(512)S(1)} %broadcast_in_dim.8), kind=kOutput, calls=%fused_computation.5 | convolution fusion | flops 402980864 | bytes 1837056 | tf_op jit(solution)/shard_map/crk,ckn->crn/dot_general | solution.py:32
  75.7 0.0 all-gather.5.cloned.1.call-update
  75.7 27.0 %all-gather.5.cloned.1.call-done = f32[1,512,512]{2,1,0:T(8,128)} async-done(((f32[1,128,512]{2,1,0:T(8,128)}), f32[1,512,512]{2,1,0:T(8,128)}) %all-gather.5.cloned.1.call-update) | async-done | bytes 1048592 | tf_op jit(solution)/shard_map/all_gather | solution.py:33
  102.8 2.2 %convolution_bitcast_fusion.1 = f32[1,128,512]{1,2,0:T(8,128)S(1)} fusion(f32[1,512,512]{2,1,0:T(8,128)} %all-gather.5.cloned.1.call-done, f32[1,128,512]{2,1,0:T(8,128)S(1)} %copy-done.1), kind=kOutput, calls=%fused_computation.1 | convolution fusion | flops 402653184 | bytes 1572864 | tf_op jit(solution)/shard_map/crn,cmn->crm/dot_general | solution.py:34
  105.0 0.8 copy.11
  105.8 0.0 copy-done.2
Async XLA Ops:
  7.2 61.7 %copy-start.3 = (s32[1,8]{1,0:T(1,128)S(1)}, s32[1,8]{1,0:T(1,128)}, u32[]{:S(2)}) copy-start(s32[1,8]{1,0:T(1,128)} %param.6) | copy-start | bytes 100
  7.2 60.3 %all-gather.3.cloned.1.call-start = ((), (), s32[]{:S(2)}) async-start(), calls=%async_computation | async-start | bytes 1081344 | tf_op jit(solution)/shard_map/all_gather | solution.py:28
  7.9 94.8 %all-gather.5.cloned.1.call-start = ((), (), s32[]{:S(2)}) async-start(), calls=%async_computation.1 | async-start | bytes 1310720 | tf_op jit(solution)/shard_map/all_gather | solution.py:33
  72.2 1.9 %copy-start = (f32[1,512,512]{2,1,0:T(8,128)S(1)}, f32[1,512,512]{2,1,0:T(8,128)}, u32[]{:S(2)}) copy-start(f32[1,512,512]{2,1,0:T(8,128)} %param.8) | copy-start | bytes 3145732
  72.2 1.9 %copy-start.1 = (f32[1,128,512]{2,1,0:T(8,128)S(1)}, f32[1,128,512]{2,1,0:T(8,128)}, u32[]{:S(2)}) copy-start(f32[1,128,512]{2,1,0:T(8,128)} %param.9) | copy-start | bytes 786436
  74.1 31.7 %copy-start.2 = (f32[128,512]{1,0:T(8,128)}, f32[128,512]{1,0:T(8,128)S(1)}, u32[]{:S(2)}) copy-start(f32[128,512]{1,0:T(8,128)S(1)} %fusion) | copy-start | bytes 786436
Sparse Core Ops, SparseCore 0:
  11.0 56.4 all-gather.2
  75.8 26.8 all-gather.4
where the time goes:
time: 113 us
  waiting for transfers between devices  84.2 us (75%)
  between operations  14.2 us (13%)
  matrix products  8.54 us (8%)
  local copies, waits for them, and re-layouts  5.04 us (4%)
    all_gather x1, waiting for transfers between devices, on_device(): lax.all_gather(root_inverse, ('leaf', 'grp'), axis=0, tiled=True)  56.4 us
    all_gather x1, waiting for transfers between devices, on_device(): q_full = lax.all_gather(q_rows, 'grp', axis=1, tiled=True)  27 us
    dot_general x1, matrix products, on_device(): jnp.einsum('crn,ckn->crk', diag_inverse_t, masked_factor, precision=highest)  2.29 us
  transfers between devices with their start and end apart: 2, of which 2 were waited for; matrix products, arithmetic and copies ran while one was open for 3% of the time, Pallas kernels for 0%

commit v1 on v0

v1 whole, which is shorter than its diff:
```python
import functools

import jax
import jax.numpy as jnp
from jax import lax
from jax.experimental import pallas as pl
from jax.experimental.pallas import tpu as pltpu
from jax.sharding import PartitionSpec as P

B = 64
CHUNKS = 4
MESH = pl.DeviceIdType.MESH
BF16 = jnp.bfloat16
F32 = jnp.float32


def halves(x):
    high = x.astype(BF16)
    return high, (x - high.astype(F32)).astype(BF16)


def dot(a, b, transpose_b=False):
    dims = (((1,), (1 if transpose_b else 0,)), ((), ()))
    return lax.dot_general(a, b, dims, preferred_element_type=F32)


def dot3(a, b, transpose_b=False):
    (ah, al), (bh, bl) = a, b
    return dot(ah, bh, transpose_b) + (dot(al, bh, transpose_b) + dot(ah, bl, transpose_b))


def kernel(
    leaves, groups,
    tiles, valid, root, factor, diag_t, cross_out, closing_out,
    d_all, root_all, f_all, closing,
    local_sem, root_recv, root_zsend, root_psend, root_tsend, d_recv, d_send,
):
    leaf = lax.axis_index("leaf")
    g = lax.axis_index("grp")
    chips = leaves // 2
    chip, core = leaf // 2, lax.rem(leaf, 2)
    twin = chip * 2 + (1 - core)
    listed = tiles.shape[1]
    rows, width = diag_t.shape
    total = root.shape[1]
    part = rows // CHUNKS

    def leaf_of(step):
        return lax.rem(chip + step, chips) * 2 + core

    barrier = pltpu.get_barrier_semaphore()

    @pl.when(g > 0)
    def _():
        pl.semaphore_signal(barrier, inc=1, device_id={"grp": g - 1}, device_id_type=MESH)

    @pl.when(g < groups - 1)
    def _():
        pl.semaphore_signal(barrier, inc=1, device_id={"grp": g + 1}, device_id_type=MESH)

    pl.semaphore_signal(barrier, inc=1, device_id={"leaf": twin}, device_id_type=MESH)
    for step in range(1, chips):
        pl.semaphore_signal(barrier, inc=1, device_id={"leaf": leaf_of(step)}, device_id_type=MESH)

    mine = leaf * groups + g
    copy_d = pltpu.make_async_copy(diag_t, d_all.at[g], local_sem.at[0])
    copy_f = pltpu.make_async_copy(factor, f_all, local_sem.at[1])
    copy_r = pltpu.make_async_copy(root, root_all.at[mine], local_sem.at[2])
    copy_d.start()
    copy_f.start()
    copy_r.start()
    near = jnp.where(g > 0, 1, 0) + jnp.where(g < groups - 1, 1, 0)
    pl.semaphore_wait(barrier, near + chips)

    def root_z(way, owner, own):
        slot = leaf * groups + owner
        return pltpu.make_async_remote_copy(
            src_ref=root if own else root_all.at[slot],
            dst_ref=root_all.at[slot],
            send_sem=root_zsend.at[way, owner],
            recv_sem=root_recv.at[slot],
            device_id={"grp": g + 1 if way == 0 else g - 1},
            device_id_type=MESH,
        )

    def root_plane(step, owner, own):
        slot = leaf * groups + owner
        return pltpu.make_async_remote_copy(
            src_ref=root if own else root_all.at[slot],
            dst_ref=root_all.at[slot],
            send_sem=root_psend.at[step, owner],
            recv_sem=root_recv.at[slot],
            device_id={"leaf": twin if step == 0 else leaf_of(step)},
            device_id_type=MESH,
        )

    def root_twin(step, owner):
        slot = leaf_of(step) * groups + owner
        return pltpu.make_async_remote_copy(
            src_ref=root_all.at[slot],
            dst_ref=root_all.at[slot],
            send_sem=root_tsend.at[step, owner],
            recv_sem=root_recv.at[slot],
            device_id={"leaf": twin},
            device_id_type=MESH,
        )

    def root_arrived(slot):
        pltpu.make_async_remote_copy(
            src_ref=root_all.at[slot],
            dst_ref=root_all.at[slot],
            send_sem=root_tsend.at[0, 0],
            recv_sem=root_recv.at[slot],
            device_id={"leaf": twin},
            device_id_type=MESH,
        ).wait_recv()

    def d_copy(way, owner, c, own):
        piece = pl.ds(c * part, part)
        return pltpu.make_async_remote_copy(
            src_ref=diag_t.at[piece] if own else d_all.at[owner, piece],
            dst_ref=d_all.at[owner, piece],
            send_sem=d_send.at[way, owner, c],
            recv_sem=d_recv.at[owner, c],
            device_id={"grp": g + 1 if way == 0 else g - 1},
            device_id_type=MESH,
        )

    def d_arrived(owner, c):
        piece = pl.ds(c * part, part)
        pltpu.make_async_remote_copy(
            src_ref=d_all.at[owner, piece],
            dst_ref=d_all.at[owner, piece],
            send_sem=d_send.at[0, owner, c],
            recv_sem=d_recv.at[owner, c],
            device_id={"leaf": twin},
            device_id_type=MESH,
        ).wait_recv()

    up, down = g < groups - 1, g > 0

    @pl.when(up)
    def _():
        root_z(0, g, True).start()

    @pl.when(down)
    def _():
        root_z(1, g, True).start()

    for step in list(range(1, chips)) + [0]:
        root_plane(step, g, True).start()
    for c in range(CHUNKS):
        @pl.when(up)
        def _():
            d_copy(0, g, c, True).start()

        @pl.when(down)
        def _():
            d_copy(1, g, c, True).start()

    def forward_root(step):
        for way, owner, there, onward in (
            (0, g - step, g - step >= 0, up),
            (1, g + step, g + step < groups, down),
        ):
            @pl.when(there)
            def _():
                root_arrived(leaf * groups + owner)

                @pl.when(onward)
                def _():
                    root_z(way, owner, False).start()

                for hop in list(range(1, chips)) + [0]:
                    root_plane(hop, owner, False).start()

    def forward_d(step):
        for c in range(CHUNKS):
            for way, owner, there, onward in (
                (0, g - step, g - step >= 0, up),
                (1, g + step, g + step < groups, down),
            ):
                @pl.when(there)
                def _():
                    d_arrived(owner, c)

                    @pl.when(onward)
                    def _():
                        d_copy(way, owner, c, False).start()

    row_at = lax.broadcasted_iota(jnp.int32, (listed * B, 1), 0)
    col_at = lax.broadcasted_iota(jnp.int32, (1, listed * B), 1)
    start = jnp.zeros((listed * B, 1), jnp.int32)
    keep = jnp.zeros((1, listed * B), jnp.int32)
    for k in range(listed):
        met = valid[0, k]
        column = jnp.where(met > 0, tiles[0, k] * B - k * B, -(2 * total) - listed * B)
        start = jnp.where(row_at // B == k, column, start)
        keep = jnp.where(col_at // B == k, met, keep)
    spot = lax.broadcasted_iota(jnp.int32, (listed * B, total), 1)
    pick = (start + row_at == spot).astype(F32)
    chosen = jnp.max(pick, axis=0, keepdims=True) > 0
    pick = pick.astype(BF16)

    copy_d.wait()
    d_own = d_all[g]
    d_half = halves(d_own)
    copy_f.wait()
    f_half = halves(f_all[...])
    product = dot3(d_half, f_half, True)
    product = jnp.where(keep > 0, product, 0.0)
    spread = tuple(dot(x, pick).astype(BF16) for x in halves(product))

    copy_r.wait()
    for step in range(1, groups):
        forward_root(step)
    if groups > 2:
        forward_d(1)
    order = [0]
    for away in range(1, groups):
        order += [away, -away]
    for away in order:
        owner = g + away
        @pl.when(jnp.logical_and(owner >= 0, owner < groups))
        def _():
            for step in range(1, chips):
                root_arrived(leaf_of(step) * groups + owner)
                root_twin(step, owner).start()
    for away in order:
        owner = g + away
        @pl.when(jnp.logical_and(owner >= 0, owner < groups))
        def _():
            for step in range(chips):
                other = lax.rem(chip + step, chips) * 2 + (1 - core)
                root_arrived(other * groups + owner)

    cross = jnp.zeros((rows, listed * B), F32)
    block = min(total, 512)
    for n in range(total // block):
        cols = slice(n * block, (n + 1) * block)
        source = root_all[:, :, cols].reshape(total, block)
        y = dot3(spread, halves(source))
        yh, yl = halves(jnp.where(chosen[:, cols], y, 0.0))
        cross = cross - (dot(yh, pick[:, cols], True) + dot(yl, pick[:, cols], True))
    cross_out[...] = cross
    q = halves(d_own - dot3(halves(cross), f_half))

    def close(owner):
        closing[owner] = dot3(q, halves(d_all[owner]), True)

    close(g)
    for step in range(1, groups):
        if step > 1 or groups <= 2:
            forward_d(step)
        for owner, there in ((g - step, g - step >= 0), (g + step, g + step < groups)):
            @pl.when(there)
            def _():
                close(owner)
    for h in range(groups):
        closing_out[:, h * rows:(h + 1) * rows] = closing[h]

    for h in range(groups):
        for way, goes in (
            (0, jnp.logical_and(h <= g, up)),
            (1, jnp.logical_and(h >= g, down)),
        ):
            @pl.when(goes)
            def _():
                root_z(way, h, False).wait_send()
                for c in range(CHUNKS):
                    d_copy(way, h, c, False).wait_send()
        for step in range(chips):
            root_plane(step, h, False).wait_send()
        for step in range(1, chips):
            root_twin(step, h).wait_send()


def on_device(root, tiles, valid, factor, diag_t):
    leaves, groups = lax.axis_size("leaf"), lax.axis_size("grp")
    rows, width = diag_t.shape[1:]
    part, total = root.shape
    deep = factor.shape[1]
    smem = pl.BlockSpec(memory_space=pltpu.SMEM)
    anywhere = pl.BlockSpec(memory_space=pl.ANY)
    vmem = pl.BlockSpec(memory_space=pltpu.VMEM)
    dma = pltpu.SemaphoreType.DMA
    cross, closing = pl.pallas_call(
        functools.partial(kernel, leaves, groups),
        out_shape=(
            jax.ShapeDtypeStruct((rows, deep), F32),
            jax.ShapeDtypeStruct((rows, groups * rows), F32),
        ),
        in_specs=[smem, smem, anywhere, anywhere, anywhere],
        out_specs=(vmem, vmem),
        scratch_shapes=[
            pltpu.VMEM((groups, rows, width), F32),
            pltpu.VMEM((leaves * groups, part, total), F32),
            pltpu.VMEM((deep, width), F32),
            pltpu.VMEM((groups, rows, rows), F32),
            dma((3,)),
            dma((leaves * groups,)),
            dma((2, groups)),
            dma((leaves // 2, groups)),
            dma((leaves // 2, groups)),
            dma((groups, CHUNKS)),
            dma((2, groups, CHUNKS)),
        ],
        compiler_params=pltpu.CompilerParams(
            collective_id=0, has_side_effects=True, vmem_limit_bytes=56 * 1024 * 1024
        ),
        name="selected_inverse",
    )(tiles, valid, root, factor[0], diag_t[0])
    return cross[None], closing[None]


def solution(mesh):
    in_specs = (
        P(("leaf", "grp"), None),
        P("leaf", None),
        P("leaf", None),
        P("leaf", None, None),
        P("leaf", "grp", None),
    )
    out_specs = (P("leaf", "grp", None), P("leaf", "grp", None))
    return jax.shard_map(
        on_device, mesh=mesh, in_specs=in_specs, out_specs=out_specs, check_vma=False
    )
```

time: 113 us -> 33.2 us (0.29)
  waiting for transfers between devices: 84.2 us -> 0 us
  Pallas kernels: 0 us -> 29.9 us
  between operations: 14.2 us -> 0.65 us
  matrix products: 8.54 us -> 0 us
  local copies, waits for them, and re-layouts: 5.04 us -> 2.42 us
    all_gather x2 -> x0, waiting for transfers between devices: 83.5 us -> none  [the longest x1 56.4 us: on_device(): lax.all_gather(root_inverse, ('leaf', 'grp'), axis=0, tiled=True)]
    pallas_call x0 -> x1, Pallas kernels: none -> 29.9 us  [on_device(): pl.pallas_call(functools.partial(kernel, leaves, groups), out_shape=(jax....]
    dot_general x6 -> x0, matrix products: 8.54 us -> none  [the longest x1 2.29 us: on_device(): jnp.einsum('crn,ckn->crk', diag_inverse_t, masked_factor, precision=highest)]
    another operation x2 -> x0, local copies, waits for them, and re-layouts: 2.01 us -> none
    unnamed x9 -> x4, local copies, waits for them, and re-layouts: 0.86 us -> 2.42 us
    reshape x1 -> x0, local copies, waits for them, and re-layouts: 1.42 us -> none  [pick_block(): flat_source = source.reshape(tile_count, tile_rows * tile_count * B)]
  transfers between devices with their start and end apart: 2 -> 0, of which waited for: 2 -> 0; matrix products, arithmetic and copies ran while one was open for 3% -> 0% of each run, Pallas kernels for 0% -> 0%
where the time goes in v1:
time: 33.2 us; the launch traced here: 33 us
  Pallas kernels  29.9 us (90%)
  local copies, waits for them, and re-layouts  2.42 us (7%)
  between operations  0.65 us (2%)
    pallas_call x1, Pallas kernels, on_device(): pl.pallas_call(functools.partial(kernel, leaves, groups), out_shape=(jax....  29.9 us
    unnamed x4, local copies, waits for them, and re-layouts  2.42 us

profile of v1, /device:TPU:0, one launch (start us, length us, event | category | flops | bytes accessed | tf_op | source)
XLA Modules:
  0.0 33.0 jit_solution(14300961596312848899)
XLA Ops:
  0.6 29.9 %selected_inverse.1 = (f32[128,512]{1,0:T(8,128)}, f32[128,512]{1,0:T(8,128)}) custom-call(s32[1,8]{1,0:T(1,128)} %tiles.1, s32[1,8]{1,0:T(1,128)} %valid.1, f32[16,512]{1,0:T(8,128)} %root.1, f32[512,512]{1,0:T(8,128)} %bitcast.4, f32[128,512]{1,0:T(8,128)} %bitcast.7), custom_call_target="tpu_custom_call" | custom-call | tf_op jit(solution)/shard_map/selected_inverse/pallas_call | solution.py:287
  30.6 0.0 copy-start
  30.6 1.7 %copy.9 = f32[1,128,512]{2,1,0:T(8,128)} copy(f32[1,128,512]{2,1,0:T(8,128)} %bitcast.6) | data formatting | bytes 524288
  32.3 0.0 copy-done
  32.3 0.7 %copy.10 = f32[1,128,512]{2,1,0:T(8,128)} copy(f32[1,128,512]{2,1,0:T(8,128)S(1)} %bitcast.5) | data formatting | bytes 524288
Async XLA Ops:
  30.6 1.7 %copy-start = (f32[128,512]{1,0:T(8,128)S(1)}, f32[128,512]{1,0:T(8,128)}, u32[]{:S(2)}) copy-start(f32[128,512]{1,0:T(8,128)} %get-tuple-element.5) | copy-start | bytes 786436

commit v2 on v1

--- a/solution.py
+++ b/solution.py
@@ -50,14 +50,10 @@
 
     barrier = pltpu.get_barrier_semaphore()
 
-    @pl.when(g > 0)
-    def _():
-        pl.semaphore_signal(barrier, inc=1, device_id={"grp": g - 1}, device_id_type=MESH)
-
-    @pl.when(g < groups - 1)
-    def _():
-        pl.semaphore_signal(barrier, inc=1, device_id={"grp": g + 1}, device_id_type=MESH)
-
+    for step in range(1, groups):
+        pl.semaphore_signal(
+            barrier, inc=1, device_id={"grp": lax.rem(g + step, groups)}, device_id_type=MESH
+        )
     pl.semaphore_signal(barrier, inc=1, device_id={"leaf": twin}, device_id_type=MESH)
     for step in range(1, chips):
         pl.semaphore_signal(barrier, inc=1, device_id={"leaf": leaf_of(step)}, device_id_type=MESH)
@@ -69,17 +65,15 @@
     copy_d.start()
     copy_f.start()
     copy_r.start()
-    near = jnp.where(g > 0, 1, 0) + jnp.where(g < groups - 1, 1, 0)
-    pl.semaphore_wait(barrier, near + chips)
-
-    def root_z(way, owner, own):
-        slot = leaf * groups + owner
+    pl.semaphore_wait(barrier, groups - 1 + chips)
+
+    def root_z(step):
         return pltpu.make_async_remote_copy(
-            src_ref=root if own else root_all.at[slot],
-            dst_ref=root_all.at[slot],
-            send_sem=root_zsend.at[way, owner],
-            recv_sem=root_recv.at[slot],
-            device_id={"grp": g + 1 if way == 0 else g - 1},
+            src_ref=root,
+            dst_ref=root_all.at[mine],
+            send_sem=root_zsend.at[step],
+            recv_sem=root_recv.at[mine],
+            device_id={"grp": lax.rem(g + step, groups)},
             device_id_type=MESH,
         )
 
@@ -139,14 +133,8 @@
 
     up, down = g < groups - 1, g > 0
 
-    @pl.when(up)
-    def _():
-        root_z(0, g, True).start()
-
-    @pl.when(down)
-    def _():
-        root_z(1, g, True).start()
-
+    for step in range(1, groups):
+        root_z(step).start()
     for step in list(range(1, chips)) + [0]:
         root_plane(step, g, True).start()
     for c in range(CHUNKS):
@@ -159,18 +147,10 @@
             d_copy(1, g, c, True).start()
 
     def forward_root(step):
-        for way, owner, there, onward in (
-            (0, g - step, g - step >= 0, up),
-            (1, g + step, g + step < groups, down),
-        ):
+        for owner, there in ((g - step, g - step >= 0), (g + step, g + step < groups)):
             @pl.when(there)
             def _():
                 root_arrived(leaf * groups + owner)
-
-                @pl.when(onward)
-                def _():
-                    root_z(way, owner, False).start()
-
                 for hop in list(range(1, chips)) + [0]:
                     root_plane(hop, owner, False).start()
 
@@ -214,8 +194,8 @@
     copy_r.wait()
     for step in range(1, groups):
         forward_root(step)
-    if groups > 2:
-        forward_d(1)
+    for step in range(1, groups - 1):
+        forward_d(step)
     order = [0]
     for away in range(1, groups):
         order += [away, -away]
@@ -250,7 +230,7 @@
 
     close(g)
     for step in range(1, groups):
-        if step > 1 or groups <= 2:
+        if step == groups - 1:
             forward_d(step)
         for owner, there in ((g - step, g - step >= 0), (g + step, g + step < groups)):
             @pl.when(there)
@@ -259,6 +239,8 @@
     for h in range(groups):
         closing_out[:, h * rows:(h + 1) * rows] = closing[h]
 
+    for step in range(1, groups):
+        root_z(step).wait_send()
     for h in range(groups):
         for way, goes in (
             (0, jnp.logical_and(h <= g, up)),
@@ -266,7 +248,6 @@
         ):
             @pl.when(goes)
             def _():
-                root_z(way, h, False).wait_send()
                 for c in range(CHUNKS):
                     d_copy(way, h, c, False).wait_send()
         for step in range(chips):
@@ -287,8 +268,8 @@
     cross, closing = pl.pallas_call(
         functools.partial(kernel, leaves, groups),
         out_shape=(
-            jax.ShapeDtypeStruct((rows, deep), F32),
-            jax.ShapeDtypeStruct((rows, groups * rows), F32),
+            pltpu.VMEM((rows, deep), F32),
+            pltpu.VMEM((rows, groups * rows), F32),
         ),
         in_specs=[smem, smem, anywhere, anywhere, anywhere],
         out_specs=(vmem, vmem),
@@ -299,7 +280,7 @@
             pltpu.VMEM((groups, rows, rows), F32),
             dma((3,)),
             dma((leaves * groups,)),
-            dma((2, groups)),
+            dma((groups,)),
             dma((leaves // 2, groups)),
             dma((leaves // 2, groups)),
             dma((groups, CHUNKS)),

time: 33.2 us -> 29.6 us (0.89)
  Pallas kernels: 29.9 us -> 27.4 us
  local copies, waits for them, and re-layouts: 2.42 us -> 1.41 us
    pallas_call x1, Pallas kernels: 29.9 us -> 27.4 us  [on_device(): pl.pallas_call(functools.partial(kernel, leaves, groups), out_shape=(pltp...]
    unnamed x4 -> x2, local copies, waits for them, and re-layouts: 2.42 us -> 1.41 us
where the time goes in v2:
time: 29.6 us; the launch traced here: 29.5 us
  Pallas kernels  27.4 us (93%)
  local copies, waits for them, and re-layouts  1.41 us (5%)
  between operations  0.64 us (2%)
    pallas_call x1, Pallas kernels, on_device(): pl.pallas_call(functools.partial(kernel, leaves, groups), out_shape=(pltp...  27.4 us
    unnamed x2, local copies, waits for them, and re-layouts  1.41 us

profile of v2, /device:TPU:0, one launch (start us, length us, event | category | flops | bytes accessed | tf_op | source)
XLA Modules:
  0.0 29.5 jit_solution(584093181093897207)
XLA Ops:
  0.6 27.4 %selected_inverse.1 = (f32[128,512]{1,0:T(8,128)S(1)}, f32[128,512]{1,0:T(8,128)S(1)}) custom-call(s32[1,8]{1,0:T(1,128)} %tiles.1, s32[1,8]{1,0:T(1,128)} %valid.1, f32[16,512]{1,0:T(8,128)} %root.1, f32[512,512]{1,0:T(8,128)} %bitcast.6, f32[128,512]{1,0:T(8,128)} %bitcast.7), custom_call_target="tpu_custom_call" | custom-call | tf_op jit(solution)/shard_map/selected_inverse/pallas_call | solution.py:268
  28.1 0.7 %copy.9 = f32[1,128,512]{2,1,0:T(8,128)} copy(f32[1,128,512]{2,1,0:T(8,128)S(1)} %bitcast.5) | data formatting | bytes 524288
  28.8 0.7 %copy.10 = f32[1,128,512]{2,1,0:T(8,128)} copy(f32[1,128,512]{2,1,0:T(8,128)S(1)} %bitcast.4) | data formatting | bytes 524288

commit v3 on v2

--- a/solution.py
+++ b/solution.py
@@ -9,6 +9,7 @@
 
 B = 64
 CHUNKS = 4
+FIRST = 2
 MESH = pl.DeviceIdType.MESH
 BF16 = jnp.bfloat16
 F32 = jnp.float32
@@ -137,14 +138,17 @@
         root_z(step).start()
     for step in list(range(1, chips)) + [0]:
         root_plane(step, g, True).start()
-    for c in range(CHUNKS):
-        @pl.when(up)
-        def _():
-            d_copy(0, g, c, True).start()
-
-        @pl.when(down)
-        def _():
-            d_copy(1, g, c, True).start()
+    def first_d(some):
+        for c in some:
+            @pl.when(up)
+            def _():
+                d_copy(0, g, c, True).start()
+
+            @pl.when(down)
+            def _():
+                d_copy(1, g, c, True).start()
+
+    first_d(range(FIRST))
 
     def forward_root(step):
         for owner, there in ((g - step, g - step >= 0), (g + step, g + step < groups)):
@@ -167,6 +171,11 @@
                     @pl.when(onward)
                     def _():
                         d_copy(way, owner, c, False).start()
+
+    copy_r.wait()
+    for step in range(1, groups):
+        forward_root(step)
+    first_d(range(FIRST, CHUNKS))
 
     row_at = lax.broadcasted_iota(jnp.int32, (listed * B, 1), 0)
     col_at = lax.broadcasted_iota(jnp.int32, (1, listed * B), 1)
@@ -191,11 +200,7 @@
     product = jnp.where(keep > 0, product, 0.0)
     spread = tuple(dot(x, pick).astype(BF16) for x in halves(product))
 
-    copy_r.wait()
-    for step in range(1, groups):
-        forward_root(step)
-    for step in range(1, groups - 1):
-        forward_d(step)
+    forward_d(1)
     order = [0]
     for away in range(1, groups):
         order += [away, -away]
@@ -206,6 +211,8 @@
             for step in range(1, chips):
                 root_arrived(leaf_of(step) * groups + owner)
                 root_twin(step, owner).start()
+    for step in range(2, groups - 1):
+        forward_d(step)
     for away in order:
         owner = g + away
         @pl.when(jnp.logical_and(owner >= 0, owner < groups))

time: 29.6 us -> 29.6 us (level)
  no operation moved by 1% of the time
where the time goes in v3:
time: 29.6 us; the launch traced here: 29.5 us
  Pallas kernels  27.4 us (93%)
  local copies, waits for them, and re-layouts  1.41 us (5%)
  between operations  0.64 us (2%)
    pallas_call x1, Pallas kernels, on_device(): pl.pallas_call(functools.partial(kernel, leaves, groups), out_shape=(pltp...  27.4 us
    unnamed x2, local copies, waits for them, and re-layouts  1.41 us

profile of v3, /device:TPU:0, one launch (start us, length us, event | category | flops | bytes accessed | tf_op | source)
XLA Modules:
  0.0 29.5 jit_solution(3192024718323480680)
XLA Ops:
  0.6 27.4 %selected_inverse.1 = (f32[128,512]{1,0:T(8,128)S(1)}, f32[128,512]{1,0:T(8,128)S(1)}) custom-call(s32[1,8]{1,0:T(1,128)} %tiles.1, s32[1,8]{1,0:T(1,128)} %valid.1, f32[16,512]{1,0:T(8,128)} %root.1, f32[512,512]{1,0:T(8,128)} %bitcast.6, f32[128,512]{1,0:T(8,128)} %bitcast.7), custom_call_target="tpu_custom_call" | custom-call | tf_op jit(solution)/shard_map/selected_inverse/pallas_call | solution.py:275
  28.0 0.7 %copy.9 = f32[1,128,512]{2,1,0:T(8,128)} copy(f32[1,128,512]{2,1,0:T(8,128)S(1)} %bitcast.5) | data formatting | bytes 524288
  28.8 0.7 %copy.10 = f32[1,128,512]{2,1,0:T(8,128)} copy(f32[1,128,512]{2,1,0:T(8,128)S(1)} %bitcast.4) | data formatting | bytes 524288
